TPU v7x, 32 devices: a whole 2x2x4 slice. The times are simulated.
32 devices in a mesh: dp: 32 (over z, y, x, core).
Axes of the slice: x: 2, y: 2, z: 4, core: 2. Of those that a mesh axis runs over, the one named last changes fastest.
Arguments:
- image_embed: float32 [16384, 1152], P('dp'), may hold values from -0.72 to 0.72
- text_embed: float32 [16384, 1152], P('dp'), may hold values from -0.72 to 0.72
- positives: int32 [16384], P('dp'), may hold values from 0 to 16383, as said below
Outputs:
- loss_rows: float32 [16384], P('dp')
- grad_image: float32 [16384, 1152], P('dp')
- grad_text: float32 [16384, 1152], P('dp')
Inputs may be any that keep to these rules, and one draw needn't show every extreme that they name: `positives`: the positive of image row i is text row ((b - k) mod (32)) * 512 + i mod 512, with b = i // 512 and k per row in 0 .. 3.
All inputs are finite; a program needn't handle non-finite values.
Results may differ from a plain program's by a relative error of at most 0.00015.
Values sent between devices are 32-bit elements; how exact they have to be, the bound alone decides.
A program may use at most 64 MiB of HBM per device.

v0:
```python
import functools

import jax
import jax.numpy as jnp
from jax import lax
from jax.experimental import pallas as pl
from jax.experimental.pallas import tpu as pltpu
from jax.sharding import PartitionSpec as P

MESH = pl.DeviceIdType.MESH
F32 = jnp.float32
BF16 = jnp.bfloat16
CHUNK = 256


def split(x):
    high = x.astype(BF16)
    return high, (x - high.astype(F32)).astype(BF16)


def dot(a, b, contract):
    return lax.dot_general(a, b, (((1,), (contract,)), ((), ())), preferred_element_type=F32)


def kernel(n, image, text, positives, grad_image, grad_text, loss, buf, high, low, total, places,
           send_sem, recv_sem, place_send, place_recv):
    rows = image.shape[0]
    chunk = min(CHUNK, rows)
    chunks = rows // chunk
    me = lax.axis_index("dp")
    odd = lax.rem(me, 2)
    partner = me + 1 - 2 * odd

    def at(offset):
        return lax.rem(me + offset + n, n)

    def piece(c):
        return pl.ds(pl.multiple_of(c * chunk, chunk), chunk)

    def remote(src, side, slot, c, lane, device):
        return pltpu.make_async_remote_copy(
            src_ref=src, dst_ref=buf.at[side, slot, piece(c)],
            send_sem=send_sem.at[lane, c], recv_sem=recv_sem.at[side, slot, c],
            device_id=(device,), device_id_type=MESH)

    def far_copies(c):
        return (
            remote(text.at[piece(c)], 0, 2, c, 0, at(2)),
            remote(image.at[piece(c)], 1, 2, c, 1, at(-2)),
        )

    def near_copies(c):
        return (
            remote(text.at[piece(c)], 0, 2 * odd + 1, c, 2, at(1 + 2 * odd)),
            remote(image.at[piece(c)], 1, 3 - 2 * odd, c, 3, at(2 * odd - 3)),
        )

    def forwards(c):
        return (
            remote(buf.at[0, 2, piece(c)], 0, 3 - 2 * odd, c, 4, partner),
            remote(buf.at[1, 2, piece(c)], 1, 2 * odd + 1, c, 5, partner),
        )

    def local(side, c):
        src = (text, image)[side]
        return pltpu.make_async_copy(src.at[piece(c)], buf.at[side, 0, piece(c)], recv_sem.at[side, 0, c])

    def place_copy(k):
        return pltpu.make_async_remote_copy(
            src_ref=places.at[0], dst_ref=places.at[k], send_sem=place_send.at[k],
            recv_sem=place_recv.at[k], device_id=(at(-k),), device_id_type=MESH)

    def arrived(side, k, c):
        ref = buf.at[side, k, piece(c)]
        pltpu.make_async_copy(ref, ref, recv_sem.at[side, k, c]).wait()

    for c in range(chunks):
        for side in range(2):
            local(side, c).start()
    places[0] = positives[...]

    barrier = pltpu.get_barrier_semaphore()
    for offset in (-3, -2, -1, 1, 2, 3):
        pl.semaphore_signal(barrier, inc=1, device_id=(at(offset),), device_id_type=MESH)
    pl.semaphore_wait(barrier, 6)

    for c in range(chunks):
        for copy in far_copies(c):
            copy.start()
    for c in range(chunks):
        for copy in near_copies(c):
            copy.start()
    for k in range(1, 4):
        place_copy(k).start()

    for c in range(chunks):
        for side in range(2):
            local(side, c).wait()
    for side in range(2):
        high[side], low[side] = split(buf[1 - side, 0])
    for k in range(1, 4):
        place_copy(k).wait_recv()

    grad_image[...] = jnp.zeros_like(grad_image)
    grad_text[...] = jnp.zeros_like(grad_text)
    total[...] = jnp.zeros_like(total)

    def unit(side, k, c):
        out = (grad_image, grad_text)[side]
        b_high, b_low = split(buf[side, k, piece(c), :])
        scores = (dot(high[side], b_high, 1) + dot(high[side], b_low, 1)) + dot(low[side], b_high, 1)
        logits = 10.0 * scores - 10.0
        wanted = places[0 if side == 0 else k, 0:1, piece(c)]
        block = lax.rem(me - k + n, n) if side == 0 else me
        lanes = lax.broadcasted_iota(jnp.int32, (1, chunk), 1) + c * chunk
        column = jnp.where(wanted == block * rows + lanes, lanes, -1)
        match = lax.broadcasted_iota(jnp.int32, (rows, chunk), 0) == column
        decay = jnp.exp(-jnp.abs(logits))
        inverse = 1.0 / (1.0 + decay)
        sigmoid = jnp.where(logits >= 0.0, inverse, decay * inverse)
        weight = (sigmoid - match.astype(F32)) * (10.0 / rows)
        if side == 0:
            signed = jnp.where(match, -logits, logits)
            part = jnp.maximum(signed, 0.0) + jnp.log1p(decay)
            for s in range(0, chunk, 128):
                total[...] += part[:, s:s + 128]
        w_high, w_low = split(weight)
        out[...] += (dot(w_high, b_high, 0) + dot(w_low, b_high, 0)) + dot(w_high, b_low, 0)

    def step(s, carry):
        c = s // 4
        r = lax.rem(s, 4)
        k_text = lax.rem(r * (3 - 2 * odd), 4)
        k_image = lax.rem(r * (1 + 2 * odd), 4)

        @pl.when(r > 0)
        def _():
            arrived(0, k_text, c)
            arrived(1, k_image, c)

        @pl.when(r == 2)
        def _():
            for copy in forwards(c):
                copy.start()

        unit(0, k_text, c)
        unit(1, k_image, c)
        return carry

    lax.fori_loop(0, 4 * chunks, step, 0)
    loss[...] = jnp.sum(total[...].T, axis=0, keepdims=True) * (1.0 / rows)

    for c in range(chunks):
        for copy in far_copies(c) + near_copies(c) + forwards(c):
            copy.wait_send()
    for k in range(1, 4):
        place_copy(k).wait_send()


def per_device(n, image_embed, text_embed, positives):
    rows, width = image_embed.shape
    chunks = rows // min(CHUNK, rows)
    vmem = pl.BlockSpec(memory_space=pltpu.VMEM)
    anywhere = pl.BlockSpec(memory_space=pl.ANY)
    block = jax.ShapeDtypeStruct((rows, width), F32)
    grad_image, grad_text, loss = pl.pallas_call(
        functools.partial(kernel, n),
        out_shape=(block, block, jax.ShapeDtypeStruct((1, rows), F32)),
        in_specs=[anywhere, anywhere, vmem],
        out_specs=(vmem, vmem, vmem),
        scratch_shapes=[
            pltpu.VMEM((2, 4, rows, width), F32),
            pltpu.VMEM((2, rows, width), BF16),
            pltpu.VMEM((2, rows, width), BF16),
            pltpu.VMEM((rows, 128), F32),
            pltpu.VMEM((4, 8, rows), jnp.int32),
            pltpu.SemaphoreType.DMA((6, chunks)),
            pltpu.SemaphoreType.DMA((2, 4, chunks)),
            pltpu.SemaphoreType.DMA((4,)),
            pltpu.SemaphoreType.DMA((4,)),
        ],
        compiler_params=pltpu.CompilerParams(
            collective_id=0, has_side_effects=True, vmem_limit_bytes=60 * 2**20),
        cost_estimate=pl.CostEstimate(
            flops=2 * 16 * 3 * rows * rows * width, bytes_accessed=16 * rows * width,
            transcendentals=8 * rows * rows),
    )(image_embed, text_embed, jnp.broadcast_to(positives[None, :], (8, rows)))
    return loss.reshape(rows), grad_image, grad_text


def solution(mesh):
    placed = (P("dp", None), P("dp", None), P("dp"))
    return jax.shard_map(
        functools.partial(per_device, mesh.shape["dp"]),
        mesh=mesh,
        in_specs=placed,
        out_specs=(P("dp"), P("dp", None), P("dp", None)),
        check_vma=False,
    )
```

profile of v0, /device:TPU:2, one launch (start us, length us, event | category | flops | bytes accessed | tf_op | source)
XLA Modules:
  0.0 214.1 jit_solution(6215768606943247318)
XLA Ops:
  0.6 1.3 broadcast_in_dim.2.positives
  1.9 206.1 %shard_map.58 = (f32[512,1152]{1,0:T(8,128)}, f32[512,1152]{1,0:T(8,128)}, f32[1,512]{1,0:T(1,128)}) custom-call(f32[512,1152]{1,0:T(8,128)} %image.1, f32[512,1152]{1,0:T(8,128)} %text.1, s32[8,512]{1,0:T(8,128)} %broadcast_in_dim.2.positives), custom_call_target="tpu_custom_call" | custom-call | flops 28991029248 | bytes 9437184 | tf_op jit(solution)/shard_map/pallas_call | solution.py:166
  208.0 1.3 copy.9
  209.3 0.0 copy-start
  209.3 3.4 %copy.10 = f32[512,1152]{1,0:T(8,128)} copy(f32[512,1152]{1,0:T(8,128)} %get-tuple-element.13) | data formatting | bytes 4718592
  212.7 0.0 copy-done
  212.7 1.4 copy.11
Async XLA Ops:
  209.3 3.4 %copy-start = (f32[512,1152]{1,0:T(8,128)S(1)}, f32[512,1152]{1,0:T(8,128)}, u32[]{:S(2)}) copy-start(f32[512,1152]{1,0:T(8,128)} %get-tuple-element.14) | copy-start | bytes 7077892
where the time goes:
time: 214 us
  Pallas kernels  206 us (96%)
  local copies, waits for them, and re-layouts  7.32 us (3%)
    pallas_call x1, Pallas kernels, per_device(): pl.pallas_call(functools.partial(kernel, n), out_shape=(block, block, jax...  206 us
    unnamed x5, local copies, waits for them, and re-layouts  6.03 us

commit v1 on v0

v1 whole, which is shorter than its diff:
```python
import functools

import jax
import jax.numpy as jnp
from jax import lax
from jax.experimental import pallas as pl
from jax.experimental.pallas import tpu as pltpu
from jax.sharding import PartitionSpec as P

MESH = pl.DeviceIdType.MESH
F32 = jnp.float32
BF16 = jnp.bfloat16
CHUNK = 128


def split(x):
    high = x.astype(BF16)
    return high, (x - high.astype(F32)).astype(BF16)


def dot(a, b, contract):
    return lax.dot_general(a, b, (((1,), (contract,)), ((), ())), preferred_element_type=F32)


def kernel(n, chunk, image, text, positives, grad_image, grad_text, loss, buf, three, total, places,
           send_sem, recv_sem, place_send, place_recv):
    rows = image.shape[0]
    chunks = rows // chunk
    me = lax.axis_index("dp")
    odd = lax.rem(me, 2)
    place = lax.rem(me, 4)
    partner = me + 1 - 2 * odd

    def at(offset):
        return lax.rem(me + offset + n, n)

    def piece(c):
        return pl.ds(pl.multiple_of(c * chunk, chunk), chunk)

    def remote(src, side, slot, c, lane, device):
        return pltpu.make_async_remote_copy(
            src_ref=src, dst_ref=buf.at[side, slot, piece(c)],
            send_sem=send_sem.at[lane, c], recv_sem=recv_sem.at[side, slot, c],
            device_id=(device,), device_id_type=MESH)

    def far_text(c):
        return remote(text.at[piece(c)], 0, 2, c, 0, at(2))

    def far_image(c):
        return remote(image.at[piece(c)], 1, 2, c, 1, at(-2))

    def relay_text(c):
        return remote(buf.at[0, 3, piece(c)], 0, 2, c, 6, at(-1))

    def relay_image(c):
        return remote(buf.at[1, 3, piece(c)], 1, 2, c, 6, at(1))

    def near_text(c):
        return remote(text.at[piece(c)], 0, 2 * odd + 1, c, 2, at(1 + 2 * odd))

    def near_image(c):
        return remote(image.at[piece(c)], 1, 3 - 2 * odd, c, 3, at(2 * odd - 3))

    def pass_text(c):
        return remote(buf.at[0, 2, piece(c)], 0, 3 - 2 * odd, c, 4, partner)

    def pass_image(c):
        return remote(buf.at[1, 2, piece(c)], 1, 2 * odd + 1, c, 5, partner)

    def local(side, c):
        src = (text, image)[side]
        return pltpu.make_async_copy(src.at[piece(c)], buf.at[side, 0, piece(c)], recv_sem.at[side, 0, c])

    def place_copy(k):
        return pltpu.make_async_remote_copy(
            src_ref=places.at[0], dst_ref=places.at[k], send_sem=place_send.at[k],
            recv_sem=place_recv.at[k], device_id=(at(-k),), device_id_type=MESH)

    def arrived(side, k, c):
        ref = buf.at[side, k, piece(c)]
        pltpu.make_async_copy(ref, ref, recv_sem.at[side, k, c]).wait()

    for c in range(chunks):
        for side in range(2):
            local(side, c).start()
    places[0] = jnp.broadcast_to(positives[...], places.shape[1:])

    barrier = pltpu.get_barrier_semaphore()
    for offset in (-3, -2, -1, 1, 2, 3):
        pl.semaphore_signal(barrier, inc=1, device_id=(at(offset),), device_id_type=MESH)
    pl.semaphore_wait(barrier, 6)

    for c in range(chunks):
        near_text(c).start()
        near_image(c).start()

        @pl.when(place != 3)
        def _():
            far_text(c).start()

        @pl.when(place != 0)
        def _():
            far_image(c).start()
    for k in range(1, 4):
        place_copy(k).start()

    for c in range(chunks):
        for side in range(2):
            local(side, c).wait()
    for side in range(2):
        a_high, a_low = split(buf[1 - side, 0])
        three[side] = jnp.concatenate([a_high, a_high, a_low], axis=1)

    def unit(side, parts, first=False):
        out = (grad_image, grad_text)[side]
        b_high, b_low = split(jnp.concatenate([buf[side, k, pl.ds(row, size), :] for k, row, size in parts], axis=0))
        scores = dot(three[side], jnp.concatenate([b_high, b_low, b_high], axis=1), 1)
        logits = 10.0 * scores - 10.0
        columns = []
        for k, row, size in parts:
            wanted = places[0 if side == 0 else k, 0:1, pl.ds(row, size)]
            block = lax.rem(me - k + n, n) if side == 0 else me
            lanes = lax.broadcasted_iota(jnp.int32, (1, size), 1) + row
            columns.append(jnp.where(wanted == block * rows + lanes, lanes, -1))
        column = jnp.concatenate(columns, axis=1)
        match = lax.broadcasted_iota(jnp.int32, scores.shape, 0) == column
        decay = jnp.exp(-jnp.abs(logits))
        inverse = 1.0 / (1.0 + decay)
        sigmoid = jnp.where(logits >= 0.0, inverse, decay * inverse)
        weight = (sigmoid - match.astype(F32)) * (10.0 / rows)
        w_high, w_low = split(weight)
        grad = dot(jnp.concatenate([w_high, w_low, w_high], axis=1),
                   jnp.concatenate([b_high, b_high, b_low], axis=0), 0)
        if first:
            out[...] = grad
        else:
            out[...] += grad
        if side == 0:
            signed = jnp.where(match, -logits, logits)
            part = jnp.maximum(signed, 0.0) + jnp.log1p(decay)
            folded = part[:, :128]
            for s in range(128, part.shape[1], 128):
                folded += part[:, s:s + 128]
            if first:
                total[...] = folded
            else:
                total[...] += folded

    for side in range(2):
        unit(side, [(0, 0, rows)], first=True)
    for k in range(1, 4):
        place_copy(k).wait_recv()

    early_text, early_image = 3 - 2 * odd, 1 + 2 * odd
    late_text, late_image = 1 + 2 * odd, 3 - 2 * odd

    def near_step(c):
        arrived(0, early_text, c)
        arrived(1, early_image, c)

        @pl.when(place == 2)
        def _():
            relay_text(c).start()

        @pl.when(place == 1)
        def _():
            relay_image(c).start()

    def step(c, carry):
        arrived(0, 2, c)
        pass_text(c).start()
        arrived(1, 2, c)
        pass_image(c).start()

        @pl.when(c + 1 < chunks)
        def _():
            near_step(c + 1)

        row = pl.multiple_of(c * chunk, chunk)
        arrived(0, late_text, c)
        unit(0, [(2, row, chunk), (late_text, row, chunk)])
        arrived(1, late_image, c)
        unit(1, [(2, row, chunk), (late_image, row, chunk)])

        @pl.when(c == chunks - 2)
        def _():
            unit(0, [(early_text, 0, rows)])
            unit(1, [(early_image, 0, rows)])

        return carry

    near_step(0)
    lax.fori_loop(0, chunks, step, 0)
    loss[...] = jnp.sum(total[...].T, axis=0, keepdims=True) * (1.0 / rows)

    for c in range(chunks):
        near_text(c).wait_send()
        near_image(c).wait_send()
        pass_text(c).wait_send()
        pass_image(c).wait_send()

        @pl.when(place != 3)
        def _():
            far_text(c).wait_send()

        @pl.when(place != 0)
        def _():
            far_image(c).wait_send()

        @pl.when(place == 2)
        def _():
            relay_text(c).wait_send()

        @pl.when(place == 1)
        def _():
            relay_image(c).wait_send()
    for k in range(1, 4):
        place_copy(k).wait_send()


def per_device(n, image_embed, text_embed, positives):
    rows, width = image_embed.shape
    chunk = CHUNK if rows % CHUNK == 0 and rows > CHUNK else rows // 2
    chunks = rows // chunk
    vmem = pl.BlockSpec(memory_space=pltpu.VMEM)
    anywhere = pl.BlockSpec(memory_space=pl.ANY)
    block = jax.ShapeDtypeStruct((rows, width), F32)
    grad_image, grad_text, loss = pl.pallas_call(
        functools.partial(kernel, n, chunk),
        out_shape=(block, block, jax.ShapeDtypeStruct((1, rows), F32)),
        in_specs=[anywhere, anywhere, vmem],
        out_specs=(vmem, vmem, vmem),
        scratch_shapes=[
            pltpu.VMEM((2, 4, rows, width), F32),
            pltpu.VMEM((2, rows, 3 * width), BF16),
            pltpu.VMEM((rows, 128), F32),
            pltpu.VMEM((4, 8, rows), jnp.int32),
            pltpu.SemaphoreType.DMA((7, chunks)),
            pltpu.SemaphoreType.DMA((2, 4, chunks)),
            pltpu.SemaphoreType.DMA((4,)),
            pltpu.SemaphoreType.DMA((4,)),
        ],
        compiler_params=pltpu.CompilerParams(
            collective_id=0, has_side_effects=True, vmem_limit_bytes=60 * 2**20),
        cost_estimate=pl.CostEstimate(
            flops=2 * 16 * 3 * rows * rows * width, bytes_accessed=16 * rows * width,
            transcendentals=8 * rows * rows),
    )(image_embed, text_embed, positives.reshape(1, rows))
    return loss.reshape(rows), grad_image, grad_text


def solution(mesh):
    placed = (P("dp", None), P("dp", None), P("dp"))
    return jax.shard_map(
        functools.partial(per_device, mesh.shape["dp"]),
        mesh=mesh,
        in_specs=placed,
        out_specs=(P("dp"), P("dp", None), P("dp", None)),
        check_vma=False,
    )
```

time: 214 us -> 152 us (0.71)
  the two profiles are of different devices: /device:TPU:2 before, /device:TPU:1 now
where the time goes in v1:
time: 152 us
  Pallas kernels  146 us (96%)
  local copies, waits for them, and re-layouts  6.03 us (4%)
    pallas_call x1, Pallas kernels, per_device(): pl.pallas_call(functools.partial(kernel, n, chunk), out_shape=(block, blo...  146 us
    unnamed x5, local copies, waits for them, and re-layouts  6.03 us

profile of v1, /device:TPU:1, one launch (start us, length us, event | category | flops | bytes accessed | tf_op | source)
XLA Modules:
  0.0 152.2 jit_solution(12448588839805354096)
XLA Ops:
  0.6 145.5 %shard_map.58 = (f32[512,1152]{1,0:T(8,128)}, f32[512,1152]{1,0:T(8,128)}, f32[1,512]{1,0:T(1,128)}) custom-call(f32[512,1152]{1,0:T(8,128)} %image.1, f32[512,1152]{1,0:T(8,128)} %text.1, s32[1,512]{1,0:T(1,128)} %bitcast.3), custom_call_target="tpu_custom_call" | custom-call | flops 28991029248 | bytes 9437184 | tf_op jit(solution)/shard_map/pallas_call | solution.py:228
  146.1 1.3 copy.9
  147.4 0.0 copy-start
  147.4 3.4 %copy.10 = f32[512,1152]{1,0:T(8,128)} copy(f32[512,1152]{1,0:T(8,128)} %get-tuple-element.13) | data formatting | bytes 4718592
  150.8 0.0 copy-done
  150.8 1.4 copy.11
Async XLA Ops:
  147.4 3.4 %copy-start = (f32[512,1152]{1,0:T(8,128)S(1)}, f32[512,1152]{1,0:T(8,128)}, u32[]{:S(2)}) copy-start(f32[512,1152]{1,0:T(8,128)} %get-tuple-element.14) | copy-start | bytes 7077892

commit v2 on v1

--- a/solution.py
+++ b/solution.py
@@ -90,17 +90,23 @@
         pl.semaphore_signal(barrier, inc=1, device_id=(at(offset),), device_id_type=MESH)
     pl.semaphore_wait(barrier, 6)
 
-    for c in range(chunks):
+    def send_near(c):
         near_text(c).start()
         near_image(c).start()
 
-        @pl.when(place != 3)
+    def send_far(c):
+        @pl.when((place != 3))
         def _():
             far_text(c).start()
 
-        @pl.when(place != 0)
+        @pl.when((place != 0))
         def _():
             far_image(c).start()
+
+    for c in range(chunks):
+        send_near(c)
+    for c in range(chunks):
+        send_far(c)
     for k in range(1, 4):
         place_copy(k).start()
 
@@ -111,10 +117,12 @@
         a_high, a_low = split(buf[1 - side, 0])
         three[side] = jnp.concatenate([a_high, a_high, a_low], axis=1)
 
-    def unit(side, parts, first=False):
+    def scored(side, parts):
+        b_high, b_low = split(jnp.concatenate([buf[side, k, pl.ds(row, size), :] for k, row, size in parts], axis=0))
+        return b_high, b_low, dot(three[side], jnp.concatenate([b_high, b_low, b_high], axis=1), 1)
+
+    def finished(side, parts, b_high, b_low, scores, first):
         out = (grad_image, grad_text)[side]
-        b_high, b_low = split(jnp.concatenate([buf[side, k, pl.ds(row, size), :] for k, row, size in parts], axis=0))
-        scores = dot(three[side], jnp.concatenate([b_high, b_low, b_high], axis=1), 1)
         logits = 10.0 * scores - 10.0
         columns = []
         for k, row, size in parts:
@@ -146,8 +154,13 @@
             else:
                 total[...] += folded
 
-    for side in range(2):
-        unit(side, [(0, 0, rows)], first=True)
+    def units(text_parts, image_parts, first=False):
+        a = scored(0, text_parts)
+        b = scored(1, image_parts)
+        finished(0, text_parts, *a, first)
+        finished(1, image_parts, *b, first)
+
+    units([(0, 0, rows)], [(0, 0, rows)], first=True)
     for k in range(1, 4):
         place_copy(k).wait_recv()
 
@@ -158,11 +171,11 @@
         arrived(0, early_text, c)
         arrived(1, early_image, c)
 
-        @pl.when(place == 2)
+        @pl.when((place == 2))
         def _():
             relay_text(c).start()
 
-        @pl.when(place == 1)
+        @pl.when((place == 1))
         def _():
             relay_image(c).start()
 
@@ -176,16 +189,15 @@
         def _():
             near_step(c + 1)
 
+        arrived(0, late_text, c)
+        arrived(1, late_image, c)
         row = pl.multiple_of(c * chunk, chunk)
-        arrived(0, late_text, c)
-        unit(0, [(2, row, chunk), (late_text, row, chunk)])
-        arrived(1, late_image, c)
-        unit(1, [(2, row, chunk), (late_image, row, chunk)])
-
-        @pl.when(c == chunks - 2)
-        def _():
-            unit(0, [(early_text, 0, rows)])
-            unit(1, [(early_image, 0, rows)])
+        units([(2, row, chunk), (late_text, row, chunk)], [(2, row, chunk), (late_image, row, chunk)])
+
+        @pl.when((c == chunks // 2 - 1) | (c == chunks - 2))
+        def _():
+            row = pl.multiple_of((c // (chunks // 2)) * (rows // 2), rows // 2)
+            units([(early_text, row, rows // 2)], [(early_image, row, rows // 2)])
 
         return carry
 
@@ -199,19 +211,19 @@
         pass_text(c).wait_send()
         pass_image(c).wait_send()
 
-        @pl.when(place != 3)
+        @pl.when((place != 3))
         def _():
             far_text(c).wait_send()
 
-        @pl.when(place != 0)
+        @pl.when((place != 0))
         def _():
             far_image(c).wait_send()
 
-        @pl.when(place == 2)
+        @pl.when((place == 2))
         def _():
             relay_text(c).wait_send()
 
-        @pl.when(place == 1)
+        @pl.when((place == 1))
         def _():
             relay_image(c).wait_send()
     for k in range(1, 4):
@@ -220,7 +232,7 @@
 
 def per_device(n, image_embed, text_embed, positives):
     rows, width = image_embed.shape
-    chunk = CHUNK if rows % CHUNK == 0 and rows > CHUNK else rows // 2
+    chunk = CHUNK if rows % (4 * CHUNK) == 0 else rows // 4
     chunks = rows // chunk
     vmem = pl.BlockSpec(memory_space=pltpu.VMEM)
     anywhere = pl.BlockSpec(memory_space=pl.ANY)

time: 152 us -> 142 us (0.934); the launches traced: 152 us -> 140 us
  Pallas kernels: 146 us -> 133 us
    pallas_call x1, Pallas kernels: 146 us -> 133 us  [per_device(): pl.pallas_call(functools.partial(kernel, n, chunk), out_shape=(block, blo...]
where the time goes in v2:
time: 142 us; the launch traced here: 140 us
  Pallas kernels  133 us (94%)
  local copies, waits for them, and re-layouts  6.03 us (4%)
    pallas_call x1, Pallas kernels, per_device(): pl.pallas_call(functools.partial(kernel, n, chunk), out_shape=(block, blo...  133 us
    unnamed x5, local copies, waits for them, and re-layouts  6.03 us

profile of v2, /device:TPU:1, one launch (start us, length us, event | category | flops | bytes accessed | tf_op | source)
XLA Modules:
  0.0 140.0 jit_solution(9204163901582703738)
XLA Ops:
  0.6 133.3 %shard_map.58 = (f32[512,1152]{1,0:T(8,128)}, f32[512,1152]{1,0:T(8,128)}, f32[1,512]{1,0:T(1,128)}) custom-call(f32[512,1152]{1,0:T(8,128)} %image.1, f32[512,1152]{1,0:T(8,128)} %text.1, s32[1,512]{1,0:T(1,128)} %bitcast.3), custom_call_target="tpu_custom_call" | custom-call | flops 28991029248 | bytes 9437184 | tf_op jit(solution)/shard_map/pallas_call | solution.py:240
  134.0 1.3 copy.9
  135.2 0.0 copy-start
  135.2 3.4 %copy.10 = f32[512,1152]{1,0:T(8,128)} copy(f32[512,1152]{1,0:T(8,128)} %get-tuple-element.13) | data formatting | bytes 4718592
  138.6 0.0 copy-done
  138.6 1.4 %copy.11 = f32[512,1152]{1,0:T(8,128)} copy(f32[512,1152]{1,0:T(8,128)S(1)} %copy-done) | data formatting | bytes 4718592
Async XLA Ops:
  135.2 3.4 %copy-start = (f32[512,1152]{1,0:T(8,128)S(1)}, f32[512,1152]{1,0:T(8,128)}, u32[]{:S(2)}) copy-start(f32[512,1152]{1,0:T(8,128)} %get-tuple-element.14) | copy-start | bytes 7077892

commit v3 on v2

--- a/solution.py
+++ b/solution.py
@@ -185,23 +185,24 @@
         arrived(1, 2, c)
         pass_image(c).start()
 
-        @pl.when(c + 1 < chunks)
-        def _():
-            near_step(c + 1)
+        @pl.when(c + 2 < chunks)
+        def _():
+            near_step(c + 2)
 
         arrived(0, late_text, c)
         arrived(1, late_image, c)
         row = pl.multiple_of(c * chunk, chunk)
         units([(2, row, chunk), (late_text, row, chunk)], [(2, row, chunk), (late_image, row, chunk)])
 
-        @pl.when((c == chunks // 2 - 1) | (c == chunks - 2))
-        def _():
-            row = pl.multiple_of((c // (chunks // 2)) * (rows // 2), rows // 2)
+        @pl.when((c == chunks // 2 - 2) | (c == chunks - 3))
+        def _():
+            row = pl.multiple_of((c // (chunks - 3)) * (rows // 2), rows // 2)
             units([(early_text, row, rows // 2)], [(early_image, row, rows // 2)])
 
         return carry
 
     near_step(0)
+    near_step(1)
     lax.fori_loop(0, chunks, step, 0)
     loss[...] = jnp.sum(total[...].T, axis=0, keepdims=True) * (1.0 / rows)
 

time: 142 us -> 140 us (0.986); the launches traced: 140 us -> 140 us
  no operation moved by 1% of the time
where the time goes in v3:
time: 140 us
  Pallas kernels  133 us (95%)
  local copies, waits for them, and re-layouts  6.03 us (4%)
    pallas_call x1, Pallas kernels, per_device(): pl.pallas_call(functools.partial(kernel, n, chunk), out_shape=(block, blo...  133 us
    unnamed x5, local copies, waits for them, and re-layouts  6.03 us

profile of v3, /device:TPU:1, one launch (start us, length us, event | category | flops | bytes accessed | tf_op | source)
XLA Modules:
  0.0 140.0 jit_solution(5759789766374438823)
XLA Ops:
  0.6 133.4 %shard_map.58 = (f32[512,1152]{1,0:T(8,128)}, f32[512,1152]{1,0:T(8,128)}, f32[1,512]{1,0:T(1,128)}) custom-call(f32[512,1152]{1,0:T(8,128)} %image.1, f32[512,1152]{1,0:T(8,128)} %text.1, s32[1,512]{1,0:T(1,128)} %bitcast.3), custom_call_target="tpu_custom_call" | custom-call | flops 28991029248 | bytes 9437184 | tf_op jit(solution)/shard_map/pallas_call | solution.py:241
  134.0 1.3 copy.9
  135.3 0.0 copy-start
  135.3 3.4 %copy.10 = f32[512,1152]{1,0:T(8,128)} copy(f32[512,1152]{1,0:T(8,128)} %get-tuple-element.13) | data formatting | bytes 4718592
  138.6 0.0 copy-done
  138.6 1.4 %copy.11 = f32[512,1152]{1,0:T(8,128)} copy(f32[512,1152]{1,0:T(8,128)S(1)} %copy-done) | data formatting | bytes 4718592
Async XLA Ops:
  135.3 3.4 %copy-start = (f32[512,1152]{1,0:T(8,128)S(1)}, f32[512,1152]{1,0:T(8,128)}, u32[]{:S(2)}) copy-start(f32[512,1152]{1,0:T(8,128)} %get-tuple-element.14) | copy-start | bytes 7077892
